TPU v7x, 256 devices: a whole 4x4x8 slice. The times are simulated.
256 devices in a mesh: req: 32 (over y, z), tp: 8 (over x, core).
Axes of the slice: x: 4, y: 4, z: 8, core: 2. Of those that a mesh axis runs over, the one named last changes fastest.
Arguments:
- tokens: bfloat16 [32768, 8192], P('req'), may hold values from -6 to 6
- request_adapter: int32 [32768, 1], P('req'), may hold values from 0 to 255; in each aligned block of 1024 rows (0 to 1023, 1024 to 2047, ...) at most 6 rows name the same one
- storage_position: int32 [256], replicated, may hold values from 0 to 255, each once
- key_value_weight: bfloat16 [8192, 2, 1024], P(None, None, 'tp'), may hold values from -0.0625 to 0.0625
- adapter_down_maps: bfloat16 [256, 8192, 128], P('req', 'tp'), may hold values from -0.0625 to 0.0625
- adapter_up_maps: bfloat16 [256, 2, 64, 1024], P('req', None, None, 'tp'), may hold values from -0.75 to 0.75
Outputs:
- kv_out: bfloat16 [32768, 2, 1024], P('req', None, 'tp')
Inputs may be any that keep to these rules, and one draw needn't show every extreme that they name: `request_adapter`: among the rows of one request group no adapter is named by more than 6 rows; in every draw some adapter is named by exactly 6 rows of some group, and every adapter is named somewhere. `storage_position`: each store position once. The panels of store position p are held by request group p // 8.
All inputs are finite; a program needn't handle non-finite values.
Results may differ from a plain program's by a relative error of at most 0.0049.
Values may be sent and summed in bfloat16 or wider, within the bound.
A program may use at most 128 MiB of HBM per device.

v0:
```python
import jax
import jax.numpy as jnp
from jax import lax
from jax.sharding import PartitionSpec as P


def local(
    tokens, request_adapter, storage_position, key_value_weight, adapter_down_maps, adapter_up_maps
):
    tok_rows, full_width = tokens.shape
    groups = lax.axis_size("req")
    tp_index = lax.axis_index("tp")
    local_adapters = adapter_down_maps.shape[0]
    portion_width = adapter_down_maps.shape[1]
    combined_rank = adapter_down_maps.shape[2]
    kv_local = key_value_weight.shape[2]
    adapter_count = storage_position.shape[0]
    bound_most = max(2, (4 * tok_rows + 3 * adapter_count - 1) // (3 * adapter_count))
    slot_count = local_adapters * bound_most
    chosen = request_adapter[:, 0]
    adapter_table = jnp.arange(adapter_count, dtype=jnp.int32)
    position = jnp.sum(
        jnp.where(chosen[:, None] == adapter_table[None, :], storage_position[None, :], 0), axis=1
    )
    owner_group = position // local_adapters
    sequence = jnp.arange(tok_rows, dtype=jnp.int32)
    earlier = (position[:, None] == position[None, :]) & (sequence[None, :] < sequence[:, None])
    place_rank = jnp.sum(earlier.astype(jnp.int32), axis=1)
    slot_index = position % local_adapters * bound_most + place_rank
    target = owner_group * slot_count + slot_index
    own_slice = lax.dynamic_slice_in_dim(tokens, tp_index * portion_width, portion_width, 1)
    outgoing = (
        jnp.zeros((groups * slot_count, portion_width), jnp.bfloat16).at[target].set(own_slice)
    )
    arrived = lax.all_to_all(
        outgoing.reshape(groups, slot_count, portion_width),
        "req",
        split_axis=0,
        concat_axis=0,
        tiled=True,
    )
    joined_output = arrived.reshape(groups, local_adapters, bound_most, portion_width)
    partial_value = jnp.einsum(
        "uebf,efn->uebn", joined_output, adapter_down_maps, preferred_element_type=jnp.float32
    )
    reduced_input = lax.psum(partial_value, "tp").astype(jnp.bfloat16)
    reduced_parts = reduced_input.reshape(groups, local_adapters, bound_most, 2, combined_rank // 2)
    update_rows = jnp.einsum(
        "fipst,istk->fipsk", reduced_parts, adapter_up_maps, preferred_element_type=jnp.float32
    ).astype(jnp.bfloat16)
    returned_rows = lax.all_to_all(
        update_rows.reshape(groups, slot_count, 2, kv_local),
        "req",
        split_axis=0,
        concat_axis=0,
        tiled=True,
    )
    own_delta = returned_rows.reshape(groups * slot_count, 2, kv_local)[target]
    base_proj = jnp.dot(
        tokens,
        key_value_weight.reshape(full_width, 2 * kv_local),
        preferred_element_type=jnp.float32,
    )
    return (base_proj.reshape(tok_rows, 2, kv_local) + own_delta.astype(jnp.float32)).astype(
        jnp.bfloat16
    )


def solution(mesh):
    in_specs = (
        P("req", None),
        P("req", None),
        P(),
        P(None, None, "tp"),
        P("req", "tp", None),
        P("req", None, None, "tp"),
    )
    out_specs = P("req", None, "tp")
    return jax.shard_map(local, mesh=mesh, in_specs=in_specs, out_specs=out_specs, check_vma=False)
```

profile of v0, /device:TPU:32, one launch (start us, length us, event | category | flops | bytes accessed | tf_op | source)
XLA Modules:
  0.0 170.9 jit_solution(5672941023117382854)
XLA Ops:
  0.0 0.0 copy-start
  0.0 1.2 select_reduce_fusion
  1.2 0.5 convert_reduce_fusion
  1.8 8.1 %scatter_custom_fusion = bf16[1536,1024]{1,0:T(8,128)(2,1)} fusion(s32[1024]{0:T(1024)S(1)} %bitcast.53, bf16[1024,8192]{1,0:T(8,128)(2,1)} %param.6, s32[]{:T(128)} %constant.34.clone.1, s32[]{:T(128)S(6)} %select_n.48, bf16[]{:T(256)} %constant.33.clone.1), kind=kCustom, calls=%fused_computation.10 | custom fusion | bytes 5243908 | tf_op jit(solution)/shard_map/scatter | solution.py:33
  9.9 84.8 %all_to_all.10 = bf16[32,48,1024]{2,1,0:T(8,128)(2,1)S(1)} all-to-all(bf16[32,48,1024]{2,1,0:T(8,128)(2,1)} %bitcast.48), channel_id=1, replica_groups=mesh['req'=32,'tp'=8] {'req'}, dimensions={0} | all-to-all | bytes 6291456 | tf_op jit(solution)/shard_map/all_to_all | solution.py:35
  94.7 1.7 %copy.25 = bf16[32,48,1024]{2,0,1:T(8,128)(2,1)S(1)} copy(bf16[32,48,1024]{2,1,0:T(8,128)(2,1)S(1)} %all_to_all.10) | data formatting | bytes 6291456 | tf_op jit(solution)/shard_map/all_to_all | solution.py:35
  96.4 0.0 copy-done
  96.4 0.0 copy-start.1
  96.4 1.0 fusion.12
  97.4 29.7 %all-reduce.1 = bf16[32,8,6,128]{3,0,2,1:T(8,128)(2,1)S(1)} all-reduce(f32[32,8,6,128]{3,0,2,1:T(8,128)S(1)} %fusion.12), channel_id=1, replica_groups=mesh['req'=32,'tp'=8] {'tp'}, use_global_device_ids=true, to_apply=%region_3.4 | all-reduce | flops 196608 | bytes 1179648 | tf_op jit(solution)/shard_map/psum | solution.py:46
  127.2 0.3 reshape.119
  127.5 0.0 copy-done.1
  127.5 0.3 fusion.11
  127.9 0.1 copy.27
  127.9 1.5 copy.28
  129.5 6.9 %all-to-all-start.1 = ((bf16[32,48,2,128]{3,2,1,0:T(2,128)(2,1)}), bf16[32,48,2,128]{3,2,1,0:T(2,128)(2,1)S(1)}, u32[]{:S(2)}, u32[]{:S(2)}) async-start(bf16[32,48,2,128]{3,2,1,0:T(2,128)(2,1)} %copy.28), calls=%async_computation.1 | async-start | bytes 1572864 | tf_op jit(solution)/shard_map/all_to_all | solution.py:51
  136.4 4.7 %copy.38 = bf16[1024,8,2,128]{3,1,2,0:T(8,128)(2,1)} copy(bf16[1024,8,2,128]{3,2,1,0:T(2,128)(2,1)} %bitcast.49) | data formatting | bytes 8388608
  141.1 6.4 %copy.24 = bf16[256,8192]{1,0:T(8,128)(2,1)} copy(bf16[256,8192]{0,1:T(8,128)(2,1)} %bitcast.47) | data formatting | bytes 8388608 | tf_op jit(solution)/shard_map/dot_general | solution.py:59
  147.4 9.0 %all-to-all-done.1 = bf16[32,48,2,128]{3,2,1,0:T(2,128)(2,1)S(1)} async-done(((bf16[32,48,2,128]{3,2,1,0:T(2,128)(2,1)}), bf16[32,48,2,128]{3,2,1,0:T(2,128)(2,1)S(1)}, u32[]{:S(2)}, u32[]{:S(2)}) %all-to-all-start.1) | async-done | bytes 786464 | tf_op jit(solution)/shard_map/all_to_all | solution.py:51
  156.5 3.7 %gather_fusion = bf16[1024,2,128]{2,1,0:T(2,128)(2,1)S(1)} fusion(bf16[1536,2,128]{2,1,0:T(2,128)(2,1)S(1)} %bitcast.52, s32[1024]{0:T(1024)S(1)} %broadcast_clamp_fusion), kind=kCustom, calls=%fused_computation | custom fusion | bytes 1052672 | tf_op jit(solution)/shard_map/gather | solution.py:58
  160.2 9.4 %fusion.15 = bf16[1024,2,128]{2,0,1:T(8,128)(2,1)S(1)} fusion(bf16[2,128,8192]{2,1,0:T(8,128)(2,1)} %bitcast.50, bf16[1024,8192]{1,0:T(8,128)(2,1)} %param.6, bf16[1024,2,128]{2,1,0:T(2,128)(2,1)S(1)} %gather_fusion), kind=kOutput, calls=%fused_computation.17 | convolution fusion | flops 4295753728 | bytes 22020096 | tf_op jit(solution)/shard_map/dot_general | solution.py:59
  169.5 1.3 copy.30
  (2 shorter events, 0.0 us)
Async XLA Ops:
  0.0 96.4 %copy-start = (bf16[8,1024,128]{2,1,0:T(8,128)(2,1)S(1)}, bf16[8,1024,128]{2,1,0:T(8,128)(2,1)}, u32[]{:S(2)}) copy-start(bf16[8,1024,128]{2,1,0:T(8,128)(2,1)} %param.10) | copy-start | bytes 6291460
  96.4 31.1 %copy-start.1 = (bf16[8,2,64,128]{3,2,1,0:T(8,128)(2,1)S(1)}, bf16[8,2,64,128]{3,2,1,0:T(8,128)(2,1)}, u32[]{:S(2)}) copy-start(bf16[8,2,64,128]{3,2,1,0:T(8,128)(2,1)} %param.11) | copy-start | bytes 786436
  129.5 27.0 %all-to-all-start.1 = ((bf16[32,48,2,128]{3,2,1,0:T(2,128)(2,1)}), bf16[32,48,2,128]{3,2,1,0:T(2,128)(2,1)S(1)}, u32[]{:S(2)}, u32[]{:S(2)}) async-start(bf16[32,48,2,128]{3,2,1,0:T(2,128)(2,1)} %copy.28), calls=%async_computation.1 | async-start | bytes 1572864 | tf_op jit(solution)/shard_map/all_to_all | solution.py:51
where the time goes:
time: 172 us; the launch traced here: 171 us
  blocking collectives  115 us (67%)
  local copies, waits for them, and re-layouts  27.9 us (16%)
  matrix products  10.7 us (6%)
  waiting for transfers between devices  9.03 us (5%)
  starting transfers between devices  6.86 us (4%)
  other arithmetic  1.78 us (1%)
    all_to_all x1, blocking collectives, local(): lax.all_to_all(outgoing.reshape(groups, slot_count, portion_width), 'req'...  84.8 us
    psum x1, blocking collectives, local(): reduced_input = lax.psum(partial_value, 'tp').astype(jnp.bfloat16)  29.7 us
    dot_general x1, matrix products, local(): jnp.dot(tokens, key_value_weight.reshape(full_width, 2 * kv_local), prefe...  9.36 us
    all_to_all x1, waiting for transfers between devices, local(): lax.all_to_all(update_rows.reshape(groups, slot_count, 2, kv_local), 'req...  9.03 us
    scatter x1, local copies, waits for them, and re-layouts, local(): jnp.zeros((groups * slot_count, portion_width), jnp.bfloat16).at[target]  8.06 us
    all_to_all x1, starting transfers between devices, local(): lax.all_to_all(update_rows.reshape(groups, slot_count, 2, kv_local), 'req...  6.86 us
    dot_general x1, local copies, waits for them, and re-layouts, local(): jnp.dot(tokens, key_value_weight.reshape(full_width, 2 * kv_local), prefe...  6.37 us
    unnamed x5, local copies, waits for them, and re-layouts  4.71 us
  transfers between devices with their start and end apart: 1, of which 1 were waited for; matrix products, arithmetic and copies ran while one was open for 6% of the time, Pallas kernels for 0%

commit v1 on v0

v1 whole, which is shorter than its diff:
```python
import functools

import jax
import jax.numpy as jnp
from jax import lax
from jax.experimental import pallas as pl
from jax.experimental.pallas import tpu as pltpu
from jax.sharding import PartitionSpec as P

MESH = pl.DeviceIdType.MESH
NY, NZ, NT = 4, 8, 8
ORDER = (4, 0, 3, 5, 2, 6, 1, 7)
CHUNKS = len(ORDER) // 2
LOCAL, MOST = 8, 6
PAIR = LOCAL * MOST
SLOTS = 192
BF16, F32 = jnp.bfloat16, jnp.float32


def dot(a, b):
    return jnp.dot(a, b, preferred_element_type=F32)


def kernel(
    tgt_row, tgt_col, code, up, tokens, weight, down, out,
    x, tok, wbuf, w32, amaps, umat, acc,
    packed, meta_out, zin, meta_in, yout, yin, part, rs_in, gath, dout, rin, zret, fin,
    x_sem, a_sem, tok_sem, w_sem,
    z_ss, z_rs, m_ss, m_rs, y_ss, y_rs, r_ss, r_rs, g_ss, g_rs, yr_ss, yr_rs, zr_ss, zr_rs,
):
    group = lax.axis_index("req")
    t = lax.axis_index("tp")
    y, z = group // NZ, group % NZ
    rows, width = x.shape
    full = tokens.shape[1]
    steps = full // width

    def at_z(offset):
        return (y * NZ + lax.rem(z + offset + NZ, NZ), t)

    def at_y(offset):
        return (lax.rem(y + offset + NY, NY) * NZ + z, t)

    def at_t(offset):
        return (group, lax.rem(t + offset, NT))

    barrier = pltpu.get_barrier_semaphore()
    peers = [at_z(d) for d in range(1, NZ)] + [at_y(d) for d in range(1, NY)]
    peers += [at_t(d) for d in range(1, NT)]
    for peer in peers:
        pl.semaphore_signal(barrier, inc=1, device_id=peer, device_id_type=MESH)

    x_copy = pltpu.make_async_copy(
        tokens.at[:, pl.ds(pl.multiple_of(t * width, width), width)], x, x_sem
    )
    x_copy.start()
    a_copy = pltpu.make_async_copy(down, amaps, a_sem)

    def base_copies(step, slot):
        return (
            pltpu.make_async_copy(
                tokens.at[:, pl.ds(pl.multiple_of(step * width, width), width)],
                tok.at[slot], tok_sem.at[slot],
            ),
            pltpu.make_async_copy(
                weight.at[pl.ds(pl.multiple_of(step * 2 * width, 2 * width), 2 * width), :],
                wbuf.at[slot], w_sem.at[slot],
            ),
        )

    def remote(src, dst, ss, rs, peer):
        return pltpu.make_async_remote_copy(
            src_ref=src, dst_ref=dst, send_sem=ss, recv_sem=rs, device_id=peer, device_id_type=MESH
        )

    sent = []
    z_copies, y_copies, r_copies, g_copies, yr_copies, zr_copies = {}, {}, {}, {}, {}, {}

    def pack(k):
        slot_id = lax.broadcasted_iota(jnp.int32, (2 * SLOTS, rows), 0) + 2 * k * SLOTS
        pick = jnp.where(slot_id == tgt_row[...], 1.0, 0.0).astype(BF16)
        codes = lax.dot_general(
            code[...], pick, (((1,), (1,)), ((), ())), preferred_element_type=F32
        )
        for i in range(2):
            q = 2 * k + i
            dst = zin if ORDER[q] == 0 else packed
            mdst = meta_in if ORDER[q] == 0 else meta_out
            mdst[q, :, 0:SLOTS] = codes[:, i * SLOTS : (i + 1) * SLOTS]
        for n in range(width // 256):
            cols = slice(n * 256, (n + 1) * 256)
            block = dot(pick, x[:, cols]).astype(BF16)
            for i in range(2):
                q = 2 * k + i
                dst = zin if ORDER[q] == 0 else packed
                dst[q, :, cols] = block[i * SLOTS : (i + 1) * SLOTS]
        for i in range(2):
            q = 2 * k + i
            if ORDER[q] == 0:
                continue
            peer = at_z(ORDER[q])
            pair = (
                remote(meta_out.at[q], meta_in.at[q], m_ss.at[q], m_rs.at[q], peer),
                remote(packed.at[q], zin.at[q], z_ss.at[q], z_rs.at[q], peer),
            )
            for copy in pair:
                copy.start()
                sent.append(copy)
            z_copies[q] = pair

    def repack(k):
        for i in range(2):
            q = 2 * k + i
            for copy in z_copies.get(q, ()):
                copy.wait_recv()
            want = lax.broadcasted_iota(jnp.int32, (NY * PAIR, SLOTS), 0).astype(F32) + 1.0
            pick = jnp.where(want == meta_in[q, 0:1, 0:SLOTS], 1.0, 0.0).astype(BF16)
            for n in range(width // 256):
                cols = slice(n * 256, (n + 1) * 256)
                block = dot(pick, zin[q, :, cols]).astype(BF16)
                for d in range(NY):
                    dst = yin if d == 0 else yout
                    dst[k, d, i * PAIR : (i + 1) * PAIR, cols] = block[d * PAIR : (d + 1) * PAIR]
        for d in range(1, NY):
            copy = remote(
                yout.at[k, d], yin.at[k, d], y_ss.at[k, d - 1], y_rs.at[k, d - 1], at_y(d)
            )
            copy.start()
            sent.append(copy)
            y_copies[k, d] = copy

    def adapter_of(shape):
        r = lax.broadcasted_iota(jnp.int32, shape, 0)
        return (r % PAIR) // MOST

    chunk_rows = 2 * NY * PAIR

    def project(k):
        for d in range(1, NY):
            y_copies[k, d].wait_recv()
        mine = adapter_of((chunk_rows, 128))

        def body(h, total):
            rhs = jnp.concatenate([amaps[2 * h], amaps[2 * h + 1]], axis=1)
            full_sum = dot(yin[k].reshape(chunk_rows, width), rhs)
            total = total + jnp.where(mine == 2 * h, full_sum[:, :128], 0.0)
            return total + jnp.where(mine == 2 * h + 1, full_sum[:, 128:], 0.0)

        total = lax.fori_loop(0, LOCAL // 2, body, jnp.zeros((chunk_rows, 128), F32))
        part[k] = total.reshape(NT, chunk_rows // NT, 128)
        for d in range(1, NT):
            peer = lax.rem(t + d, NT)
            copy = remote(
                part.at[k, peer], rs_in.at[k, d - 1], r_ss.at[k, d - 1], r_rs.at[k, d - 1], at_t(d)
            )
            copy.start()
            sent.append(copy)
            r_copies[k, d] = copy

    def reduce(k):
        for d in range(1, NT):
            r_copies[k, d].wait_recv()
        total = part[k, t]
        for d in range(1, NT):
            total = total + rs_in[k, d - 1]
        gath[k, t] = total
        for d in range(1, NT):
            copy = remote(
                gath.at[k, t], gath.at[k, t], g_ss.at[k, d - 1], g_rs.at[k, d - 1], at_t(d)
            )
            copy.start()
            sent.append(copy)
            g_copies[k, d] = copy

    def expand(k):
        for d in range(1, NT):
            g_copies[k, d].wait_recv()
        mine = adapter_of((chunk_rows, 128))
        shrunk = gath[k].reshape(chunk_rows, 128)
        spread = jnp.concatenate(
            [jnp.where(mine == e, shrunk, 0.0).astype(BF16) for e in range(LOCAL)], axis=1
        )
        delta = dot(spread, umat[...]).astype(BF16)
        for d in range(NY):
            dst = rin if d == 0 else dout
            dst[k, d] = delta[d * 2 * PAIR : (d + 1) * 2 * PAIR]
        for d in range(1, NY):
            copy = remote(
                dout.at[k, d], rin.at[k, d], yr_ss.at[k, d - 1], yr_rs.at[k, d - 1], at_y(-d)
            )
            copy.start()
            sent.append(copy)
            yr_copies[k, d] = copy

    def unpack(k):
        for d in range(1, NY):
            yr_copies[k, d].wait_recv()
        for i in range(2):
            q = 2 * k + i
            have = jnp.transpose(meta_in[q])[0:SLOTS, 0:1]
            want = lax.broadcasted_iota(jnp.int32, (SLOTS, NY * PAIR), 1).astype(F32) + 1.0
            pick = jnp.where(want == have, 1.0, 0.0).astype(BF16)
            block = jnp.concatenate(
                [rin[k, d, i * PAIR : (i + 1) * PAIR, :] for d in range(NY)], axis=0
            )
            dst = fin if ORDER[q] == 0 else zret
            dst[q] = dot(pick, block).astype(BF16)
            if ORDER[q] == 0:
                continue
            copy = remote(zret.at[q], fin.at[q], zr_ss.at[q], zr_rs.at[q], at_z(-ORDER[q]))
            copy.start()
            sent.append(copy)
            zr_copies[q] = copy

    tile = 256

    def collect(k, last):
        for q in (2 * k, 2 * k + 1):
            if q in zr_copies:
                zr_copies[q].wait_recv()

        def body(r, carry):
            span = pl.ds(pl.multiple_of(r * tile, tile), tile)
            total = acc[span, :]
            for q in (2 * k, 2 * k + 1):
                slot_id = lax.broadcasted_iota(jnp.int32, (tile, SLOTS), 1) + q * SLOTS
                pick = jnp.where(slot_id == tgt_col[span, :], 1.0, 0.0).astype(BF16)
                total = total + dot(pick, fin[q])
            if last:
                out[span, :] = total.astype(BF16)
            else:
                acc[span, :] = total
            return carry

        lax.fori_loop(0, rows // tile, body, 0)

    def base():
        acc[...] = jnp.zeros_like(acc)

        def step(s, carry):
            slot = lax.rem(s, 2)
            for copy in base_copies(s, slot):
                copy.wait()

            @pl.when(s + 1 < steps)
            def _():
                for copy in base_copies(s + 1, 1 - slot):
                    copy.start()

            w32[...] = wbuf[slot].astype(F32)
            rhs = jnp.concatenate(
                [w32[pl.ds(j, width, stride=2), :].astype(BF16) for j in range(2)], axis=1
            )

            def body(r, c):
                span = pl.ds(pl.multiple_of(r * tile, tile), tile)
                acc[span, :] += dot(tok[slot, span, :], rhs)
                return c

            lax.fori_loop(0, rows // tile, body, 0)
            return carry

        lax.fori_loop(0, steps, step, 0)

    rank_row = lax.broadcasted_iota(jnp.int32, up.shape, 0) % 128
    umat[:, 0:128] = jnp.where(rank_row < 64, up[...].astype(F32), 0.0).astype(BF16)
    umat[:, 128:256] = jnp.where(rank_row < 64, 0.0, up[...].astype(F32)).astype(BF16)

    x_copy.wait()
    a_copy.start()
    for copy in base_copies(0, 0):
        copy.start()
    pl.semaphore_wait(barrier, len(peers))
    for k in range(CHUNKS):
        pack(k)
    base()
    a_copy.wait()
    for k in (0, 1):
        repack(k)
        project(k)
        reduce(k)
        expand(k)
        unpack(k)
    repack(2)
    project(2)
    repack(3)
    reduce(2)
    project(3)
    expand(2)
    reduce(3)
    unpack(2)
    expand(3)
    collect(0, False)
    unpack(3)
    collect(1, False)
    collect(2, False)
    collect(3, True)
    for copy in sent:
        copy.wait_send()


def local(
    tokens, request_adapter, storage_position, key_value_weight, adapter_down_maps, adapter_up_maps
):
    rows, full = tokens.shape
    width = adapter_down_maps.shape[1]
    kv = key_value_weight.shape[2]
    adapters = storage_position.shape[0]
    group = lax.axis_index("req")
    y, z = group // NZ, group % NZ
    chosen = request_adapter[:, 0]
    table = jnp.arange(adapters, dtype=jnp.int32)
    position = jnp.sum(
        jnp.where(chosen[:, None] == table[None, :], storage_position[None, :], 0), axis=1
    )
    owner = position // LOCAL
    y_off = (owner // NZ - y + NY) % NY
    z_off = (owner % NZ - z + NZ) % NZ
    seq = jnp.arange(rows, dtype=jnp.int32)
    earlier = seq[None, :] < seq[:, None]
    rank = jnp.sum(((position[:, None] == position[None, :]) & earlier).astype(jnp.int32), axis=1)
    slot = jnp.sum(((z_off[:, None] == z_off[None, :]) & earlier).astype(jnp.int32), axis=1)
    turn = jnp.zeros_like(z_off)
    for q, offset in enumerate(ORDER):
        turn = jnp.where(z_off == offset, q, turn)
    target = turn * SLOTS + slot
    code = (y_off * PAIR + position % LOCAL * MOST + rank + 1).astype(BF16)
    code = jnp.broadcast_to(code[None, :], (8, rows))

    chunk = 2 * NY * PAIR
    vmem = pl.BlockSpec(memory_space=pltpu.VMEM)
    hbm = pl.BlockSpec(memory_space=pl.ANY)
    dma = pltpu.SemaphoreType.DMA
    result = pl.pallas_call(
        kernel,
        out_shape=jax.ShapeDtypeStruct((rows, 2 * kv), BF16),
        in_specs=[vmem, vmem, vmem, vmem, hbm, hbm, hbm],
        out_specs=vmem,
        scratch_shapes=[
            pltpu.VMEM((rows, width), BF16),
            pltpu.VMEM((2, rows, width), BF16),
            pltpu.VMEM((2, 2 * width, kv), BF16),
            pltpu.VMEM((2 * width, kv), F32),
            pltpu.VMEM(adapter_down_maps.shape, BF16),
            pltpu.VMEM((LOCAL * 128, 2 * kv), BF16),
            pltpu.VMEM((rows, 2 * kv), F32),
            pltpu.VMEM((NZ, SLOTS, width), BF16),
            pltpu.VMEM((NZ, 8, 256), F32),
            pltpu.VMEM((NZ, SLOTS, width), BF16),
            pltpu.VMEM((NZ, 8, 256), F32),
            pltpu.VMEM((CHUNKS, NY, 2 * PAIR, width), BF16),
            pltpu.VMEM((CHUNKS, NY, 2 * PAIR, width), BF16),
            pltpu.VMEM((CHUNKS, NT, chunk // NT, 128), F32),
            pltpu.VMEM((CHUNKS, NT - 1, chunk // NT, 128), F32),
            pltpu.VMEM((CHUNKS, NT, chunk // NT, 128), F32),
            pltpu.VMEM((CHUNKS, NY, 2 * PAIR, 2 * kv), BF16),
            pltpu.VMEM((CHUNKS, NY, 2 * PAIR, 2 * kv), BF16),
            pltpu.VMEM((NZ, SLOTS, 2 * kv), BF16),
            pltpu.VMEM((NZ, SLOTS, 2 * kv), BF16),
            dma, dma, dma((2,)), dma((2,)),
            dma((NZ,)), dma((NZ,)), dma((NZ,)), dma((NZ,)),
            dma((CHUNKS, NY - 1)), dma((CHUNKS, NY - 1)),
            dma((CHUNKS, NT - 1)), dma((CHUNKS, NT - 1)),
            dma((CHUNKS, NT - 1)), dma((CHUNKS, NT - 1)),
            dma((CHUNKS, NY - 1)), dma((CHUNKS, NY - 1)),
            dma((NZ,)), dma((NZ,)),
        ],
        compiler_params=pltpu.CompilerParams(
            collective_id=0, has_side_effects=True, vmem_limit_bytes=56 * 2**20
        ),
        cost_estimate=pl.CostEstimate(
            flops=12_000_000_000, bytes_accessed=24_000_000, transcendentals=0
        ),
    )(
        target[None, :], target[:, None], code,
        adapter_up_maps.reshape(LOCAL * 128, kv),
        tokens, key_value_weight.reshape(2 * full, kv), adapter_down_maps,
    )
    return result.reshape(rows, 2, kv)


def solution(mesh):
    in_specs = (
        P("req", None),
        P("req", None),
        P(),
        P(None, None, "tp"),
        P("req", "tp", None),
        P("req", None, None, "tp"),
    )
    out_specs = P("req", None, "tp")
    return jax.shard_map(local, mesh=mesh, in_specs=in_specs, out_specs=out_specs, check_vma=False)
```

time: 172 us -> 144 us (0.84); the launches traced: 171 us -> 141 us
  Pallas kernels: 0 us -> 133 us
  blocking collectives: 115 us -> 0 us
  local copies, waits for them, and re-layouts: 27.9 us -> 3.01 us
  matrix products: 10.7 us -> 0 us
  waiting for transfers between devices: 9.03 us -> 0 us
  starting transfers between devices: 6.86 us -> 0 us
  other arithmetic: 1.78 us -> 4.57 us
    pallas_call x0 -> x1, Pallas kernels: none -> 133 us  [local(): pl.pallas_call(kernel, out_shape=jax.ShapeDtypeStruct((rows, 2 * kv), BF1...]
    all_to_all x1 -> x0, blocking collectives: 84.8 us -> none  [local(): lax.all_to_all(outgoing.reshape(groups, slot_count, portion_width), 'req'...]
    psum x1 -> x0, blocking collectives: 29.7 us -> none  [local(): reduced_input = lax.psum(partial_value, 'tp').astype(jnp.bfloat16)]
    dot_general x3 -> x0, matrix products: 10.7 us -> none  [the longest x1 9.36 us: local(): jnp.dot(tokens, key_value_weight.reshape(full_width, 2 * kv_local), prefe...]
    all_to_all x1 -> x0, waiting for transfers between devices: 9.03 us -> none  [local(): lax.all_to_all(update_rows.reshape(groups, slot_count, 2, kv_local), 'req...]
    scatter x1 -> x0, local copies, waits for them, and re-layouts: 8.06 us -> none  [local(): jnp.zeros((groups * slot_count, portion_width), jnp.bfloat16).at[target]]
    all_to_all x1 -> x0, starting transfers between devices: 6.86 us -> none  [local(): lax.all_to_all(update_rows.reshape(groups, slot_count, 2, kv_local), 'req...]
    dot_general x1 -> x0, local copies, waits for them, and re-layouts: 6.37 us -> none  [local(): jnp.dot(tokens, key_value_weight.reshape(full_width, 2 * kv_local), prefe...]
  transfers between devices with their start and end apart: 1 -> 0, of which waited for: 1 -> 0; matrix products, arithmetic and copies ran while one was open for 6% -> 0% of each run, Pallas kernels for 0% -> 0%
where the time goes in v1:
time: 144 us; the launch traced here: 141 us
  Pallas kernels  133 us (92%)
  other arithmetic  4.57 us (3%)
  local copies, waits for them, and re-layouts  3.01 us (2%)
    pallas_call x1, Pallas kernels, local(): pl.pallas_call(kernel, out_shape=jax.ShapeDtypeStruct((rows, 2 * kv), BF1...  133 us

profile of v1, /device:TPU:32, one launch (start us, length us, event | category | flops | bytes accessed | tf_op | source)
XLA Modules:
  0.0 141.0 jit_solution(8728190898894065185)
XLA Ops:
  0.0 1.1 select_reduce_fusion
  1.1 0.5 convert_reduce_fusion
  1.6 0.5 convert_reduce_fusion.1
  2.1 0.2 copy.22
  2.4 0.2 copy.17
  2.6 1.8 %multiply_add_fusion.tgt_col = s32[1024,1]{1,0:T(8,128)} fusion(s32[1024,1]{1,0:T(8,128)S(1)} %copy.22, s32[1024,1]{1,0:T(8,128)S(1)} %copy.17, s32[]{:T(128)S(6)} %select_n.266), kind=kLoop, calls=%fused_computation.22 | loop fusion | flops 56320 | bytes 12292 | tf_op jit(solution)/shard_map/add | solution.py:326
  4.4 0.6 broadcast_in_dim.63.code
  5.0 0.7 fusion.23.tgt_row
  5.6 133.4 %shard_map.64 = bf16[1024,256]{1,0:T(8,128)(2,1)} custom-call(s32[1,1024]{1,0:T(1,128)} %fusion.23.tgt_row, s32[1024,1]{1,0:T(8,128)} %multiply_add_fusion.tgt_col, bf16[8,1024]{1,0:T(8,128)(2,1)} %broadcast_in_dim.63.code, bf16[1024,128]{1,0:T(8,128)(2,1)} %bitcast.13, bf16[1024,8192]{1,0:T(8,128)(2,1)} %tokens.1, bf16[16384,128]{1,0:T(8,128)(2,1)} %bitcast.12, ...), custom_call_target="tpu_custom_call" | custom-call | flops 12000000000 | bytes 24000000 | tf_op jit(solution)/shard_map/pallas_call | solution.py:334
  139.1 2.0 %reshape.413 = bf16[1024,2,128]{2,1,0:T(2,128)(2,1)} reshape(bf16[1024,256]{1,0:T(8,128)(2,1)} %shard_map.64) | data formatting | bytes 1048576 | tf_op jit(solution)/shard_map/reshape | solution.py:379
  (1 shorter events, 0.0 us)

commit v2 on v1

v2 whole, which is shorter than its diff:
```python
import functools

import jax
import jax.numpy as jnp
from jax import lax
from jax.experimental import pallas as pl
from jax.experimental.pallas import tpu as pltpu
from jax.sharding import PartitionSpec as P

MESH = pl.DeviceIdType.MESH
NY, NZ, NT = 4, 8, 8
ORDER = (4, 0, 3, 5, 2, 6, 1, 7)
CHUNKS = len(ORDER) // 2
LOCAL, MOST = 8, 6
PAIR = LOCAL * MOST
POOLED = (4, 3, 5)
SLOTS = 192
SIZE = tuple(SLOTS if d in POOLED else NY * PAIR for d in ORDER)
START = tuple(sum(SIZE[:q]) for q in range(NZ))
BF16, F32 = jnp.bfloat16, jnp.float32


def dot(a, b):
    return jnp.dot(a, b, preferred_element_type=F32)


def kernel(
    tgt_row, tgt_col, code, up, tokens, weight, down, out,
    x, tok, wbuf, w32, amaps, umat, acc,
    packed, meta_out, mid, meta_in, yout, yin, part, rs_in, gath, dout, rmid, zret, fin,
    x_sem, a_sem, tok_sem, w_sem,
    z_ss, z_rs, m_ss, m_rs, y_ss, y_rs, r_ss, r_rs, g_ss, g_rs, yr_ss, yr_rs, zr_ss, zr_rs,
):
    group = lax.axis_index("req")
    t = lax.axis_index("tp")
    y, z = group // NZ, group % NZ
    rows, width = x.shape
    full = tokens.shape[1]
    steps = full // width

    def at_yz(dy, dz):
        return (lax.rem(y + dy + NY, NY) * NZ + lax.rem(z + dz + NZ, NZ), t)

    def at_t(offset):
        return (group, lax.rem(t + offset, NT))

    barrier = pltpu.get_barrier_semaphore()
    pairs = {(0, d) for d in range(1, NZ)} | {(d, 0) for d in range(1, NY)}
    peers = [at_yz(d, e) for d, e in sorted(pairs)] + [at_t(d) for d in range(1, NT)]
    for peer in peers:
        pl.semaphore_signal(barrier, inc=1, device_id=peer, device_id_type=MESH)

    x_copy = pltpu.make_async_copy(
        tokens.at[:, pl.ds(pl.multiple_of(t * width, width), width)], x, x_sem
    )
    x_copy.start()
    a_copy = pltpu.make_async_copy(down, amaps, a_sem)

    def base_copies(step, slot):
        return (
            pltpu.make_async_copy(
                tokens.at[:, pl.ds(pl.multiple_of(step * width, width), width)],
                tok.at[slot], tok_sem.at[slot],
            ),
            pltpu.make_async_copy(
                weight.at[pl.ds(pl.multiple_of(step * 2 * width, 2 * width), 2 * width), :],
                wbuf.at[slot], w_sem.at[slot],
            ),
        )

    def remote(src, dst, ss, rs, peer):
        return pltpu.make_async_remote_copy(
            src_ref=src, dst_ref=dst, send_sem=ss, recv_sem=rs, device_id=peer, device_id_type=MESH
        )

    sent = []
    m_copies, z_copies, y_copies, r_copies, g_copies, yr_copies, zr_copies = ({} for _ in range(7))

    def half(d):
        return pl.ds(d * PAIR, PAIR)

    def send(table, key, copy):
        copy.start()
        sent.append(copy)
        table[key] = copy

    span = pl.ds(0, SLOTS)

    def pack(k):
        count = SIZE[2 * k] + SIZE[2 * k + 1]
        slot_id = lax.broadcasted_iota(jnp.int32, (count, rows), 0) + START[2 * k]
        pick = jnp.where(slot_id == tgt_row[...], 1.0, 0.0).astype(BF16)
        begin = (0, SIZE[2 * k])
        pooled = [i for i in range(2) if ORDER[2 * k + i] in POOLED]
        if pooled:
            codes = lax.dot_general(
                code[...], pick, (((1,), (1,)), ((), ())), preferred_element_type=F32
            )
        for i in pooled:
            meta_out[2 * k + i, :, 0:SLOTS] = codes[:, begin[i] : begin[i] + SLOTS]
        for n in range(width // 256):
            cols = slice(n * 256, (n + 1) * 256)
            block = dot(pick, x[:, cols]).astype(BF16)
            for i in range(2):
                q = 2 * k + i
                packed[q, 0 : SIZE[q], cols] = block[begin[i] : begin[i] + SIZE[q]]
                if i not in pooled:
                    land = yin if ORDER[q] == 0 else mid
                    land[q, 0:PAIR, cols] = block[begin[i] : begin[i] + PAIR]
        for i in range(2):
            q = 2 * k + i
            if i in pooled:
                peer = at_yz(0, ORDER[q])
                send(m_copies, q, remote(meta_out.at[q], meta_in.at[q], m_ss.at[q], m_rs.at[q], peer))
                send(z_copies, q, remote(
                    packed.at[q, span], mid.at[q, span], z_ss.at[q], z_rs.at[q], peer
                ))
                continue
            land = yin if ORDER[q] == 0 else mid
            for d in range(1, NY):
                send(y_copies, (q, d), remote(
                    packed.at[q, half(d)], land.at[q, half(d)],
                    y_ss.at[q, d - 1], y_rs.at[q, d - 1], at_yz(d, 0),
                ))

    def forward(k):
        for q in (2 * k, 2 * k + 1):
            for d in range(1, NY):
                y_copies[q, d].wait_recv()
            send(z_copies, q, remote(
                mid.at[q], yin.at[q], z_ss.at[q], z_rs.at[q], at_yz(0, ORDER[q])
            ))

    def repack(k):
        for q in (2 * k, 2 * k + 1):
            if ORDER[q] not in POOLED:
                continue
            m_copies[q].wait_recv()
            z_copies[q].wait_recv()
            want = lax.broadcasted_iota(jnp.int32, (NY * PAIR, SLOTS), 0).astype(F32) + 1.0
            pick = jnp.where(want == meta_in[q, 0:1, 0:SLOTS], 1.0, 0.0).astype(BF16)
            for n in range(width // 256):
                cols = slice(n * 256, (n + 1) * 256)
                block = dot(pick, mid[q, 0:SLOTS, cols]).astype(BF16)
                yin[q, 0:PAIR, cols] = block[0:PAIR]
                yout[q, :, cols] = block
            for d in range(1, NY):
                send(y_copies, (q, d), remote(
                    yout.at[q, half(d)], yin.at[q, half(d)],
                    y_ss.at[q, d - 1], y_rs.at[q, d - 1], at_yz(d, 0),
                ))

    def adapter_of(shape):
        r = lax.broadcasted_iota(jnp.int32, shape, 0)
        return (r % PAIR) // MOST

    chunk_rows = 2 * NY * PAIR

    def project(k):
        for q in (2 * k, 2 * k + 1):
            if ORDER[q] in POOLED or ORDER[q] == 0:
                for d in range(1, NY):
                    y_copies[q, d].wait_recv()
            else:
                z_copies[q].wait_recv()
        mine = adapter_of((chunk_rows, 128))

        def body(h, total):
            rhs = jnp.concatenate([amaps[2 * h], amaps[2 * h + 1]], axis=1)
            full_sum = dot(yin[2 * k : 2 * k + 2].reshape(chunk_rows, width), rhs)
            total = total + jnp.where(mine == 2 * h, full_sum[:, :128], 0.0)
            return total + jnp.where(mine == 2 * h + 1, full_sum[:, 128:], 0.0)

        total = lax.fori_loop(0, LOCAL // 2, body, jnp.zeros((chunk_rows, 128), F32))
        part[k] = total.reshape(NT, chunk_rows // NT, 128)
        for d in range(1, NT):
            peer = lax.rem(t + d, NT)
            copy = remote(
                part.at[k, peer], rs_in.at[k, d - 1], r_ss.at[k, d - 1], r_rs.at[k, d - 1], at_t(d)
            )
            copy.start()
            sent.append(copy)
            r_copies[k, d] = copy

    def reduce(k):
        for d in range(1, NT):
            r_copies[k, d].wait_recv()
        total = part[k, t]
        for d in range(1, NT):
            total = total + rs_in[k, d - 1]
        gath[k, t] = total.astype(BF16)
        for d in range(1, NT):
            copy = remote(
                gath.at[k, t], gath.at[k, t], g_ss.at[k, d - 1], g_rs.at[k, d - 1], at_t(d)
            )
            copy.start()
            sent.append(copy)
            g_copies[k, d] = copy

    def expand(k):
        for d in range(1, NT):
            g_copies[k, d].wait_recv()
        mine = adapter_of((chunk_rows, 128))
        shrunk = gath[k].reshape(chunk_rows, 128).astype(F32)
        spread = jnp.concatenate(
            [jnp.where(mine == e, shrunk, 0.0).astype(BF16) for e in range(LOCAL)], axis=1
        )
        delta = dot(spread, umat[...]).astype(BF16)
        for i in range(2):
            q = 2 * k + i
            mine = delta[i * NY * PAIR : (i + 1) * NY * PAIR]
            dout[q] = mine
            if ORDER[q] in POOLED or ORDER[q] == 0:
                land = rmid if ORDER[q] in POOLED else fin
                land[q, 0:PAIR] = mine[0:PAIR]
                for d in range(1, NY):
                    send(yr_copies, (q, d), remote(
                        dout.at[q, half(d)], land.at[q, half(d)],
                        yr_ss.at[q, d - 1], yr_rs.at[q, d - 1], at_yz(-d, 0),
                    ))
            else:
                send(zr_copies, q, remote(
                    dout.at[q], rmid.at[q], zr_ss.at[q], zr_rs.at[q], at_yz(0, -ORDER[q])
                ))

    def unpack(k):
        for q in (2 * k, 2 * k + 1):
            if ORDER[q] not in POOLED:
                continue
            for d in range(1, NY):
                yr_copies[q, d].wait_recv()
            have = jnp.transpose(meta_in[q])[0:SLOTS, 0:1]
            want = lax.broadcasted_iota(jnp.int32, (SLOTS, NY * PAIR), 1).astype(F32) + 1.0
            pick = jnp.where(want == have, 1.0, 0.0).astype(BF16)
            zret[q, 0:SLOTS] = dot(pick, rmid[q]).astype(BF16)
            send(zr_copies, q, remote(
                zret.at[q, span], fin.at[q, span], zr_ss.at[q], zr_rs.at[q], at_yz(0, -ORDER[q])
            ))

    def back(k):
        for q in (2 * k, 2 * k + 1):
            zr_copies[q].wait_recv()
            for d in range(1, NY):
                send(yr_copies, (q, d), remote(
                    rmid.at[q, half(d)], fin.at[q, half(d)],
                    yr_ss.at[q, d - 1], yr_rs.at[q, d - 1], at_yz(-d, 0),
                ))
            fin[q, 0:PAIR] = rmid[q, 0:PAIR]

    tile = 256

    def collect(k, last):
        for q in (2 * k, 2 * k + 1):
            if ORDER[q] in POOLED:
                zr_copies[q].wait_recv()
                continue
            for d in range(1, NY):
                yr_copies[q, d].wait_recv()

        def body(r, carry):
            span = pl.ds(pl.multiple_of(r * tile, tile), tile)
            total = acc[span, :]
            for q in (2 * k, 2 * k + 1):
                slot_id = lax.broadcasted_iota(jnp.int32, (tile, SIZE[q]), 1) + START[q]
                pick = jnp.where(slot_id == tgt_col[span, :], 1.0, 0.0).astype(BF16)
                total = total + dot(pick, fin[q, 0 : SIZE[q]])
            if last:
                out[span, :] = total.astype(BF16)
            else:
                acc[span, :] = total
            return carry

        lax.fori_loop(0, rows // tile, body, 0)

    def base(first, stop):
        def step(s, carry):
            slot = lax.rem(s, 2)
            for copy in base_copies(s, slot):
                copy.wait()

            @pl.when(s + 1 < steps)
            def _():
                for copy in base_copies(s + 1, 1 - slot):
                    copy.start()

            w32[...] = wbuf[slot].astype(F32)
            rhs = jnp.concatenate(
                [w32[pl.ds(j, width, stride=2), :].astype(BF16) for j in range(2)], axis=1
            )

            def body(r, c):
                span = pl.ds(pl.multiple_of(r * tile, tile), tile)
                acc[span, :] += dot(tok[slot, span, :], rhs)
                return c

            lax.fori_loop(0, rows // tile, body, 0)
            return carry

        lax.fori_loop(first, stop, step, 0)

    rank_row = lax.broadcasted_iota(jnp.int32, up.shape, 0) % 128
    umat[:, 0:128] = jnp.where(rank_row < 64, up[...].astype(F32), 0.0).astype(BF16)
    umat[:, 128:256] = jnp.where(rank_row < 64, 0.0, up[...].astype(F32)).astype(BF16)

    x_copy.wait()
    a_copy.start()
    for copy in base_copies(0, 0):
        copy.start()
    acc[...] = jnp.zeros_like(acc)
    pl.semaphore_wait(barrier, len(peers))
    pack(0)
    pack(1)
    pack(2)
    pack(3)
    base(0, 4)
    a_copy.wait()
    repack(0)
    forward(2)
    project(0)
    forward(3)
    reduce(0)
    base(4, 6)
    expand(0)
    base(6, 8)
    unpack(0)
    repack(1)
    project(1)
    reduce(1)
    expand(1)
    project(2)
    unpack(1)
    reduce(2)
    project(3)
    expand(2)
    collect(0, False)
    reduce(3)
    back(2)
    expand(3)
    collect(1, False)
    back(3)
    collect(2, False)
    collect(3, True)
    for copy in sent:
        copy.wait_send()


def local(
    tokens, request_adapter, storage_position, key_value_weight, adapter_down_maps, adapter_up_maps
):
    rows, full = tokens.shape
    width = adapter_down_maps.shape[1]
    kv = key_value_weight.shape[2]
    adapters = storage_position.shape[0]
    group = lax.axis_index("req")
    y, z = group // NZ, group % NZ
    chosen = request_adapter[:, 0]
    table = jnp.arange(adapters, dtype=jnp.int32)
    position = jnp.sum(
        jnp.where(chosen[:, None] == table[None, :], storage_position[None, :], 0), axis=1
    )
    owner = position // LOCAL
    y_off = (owner // NZ - y + NY) % NY
    z_off = (owner % NZ - z + NZ) % NZ
    seq = jnp.arange(rows, dtype=jnp.int32)
    earlier = seq[None, :] < seq[:, None]
    rank = jnp.sum(((position[:, None] == position[None, :]) & earlier).astype(jnp.int32), axis=1)
    slot = jnp.sum(((z_off[:, None] == z_off[None, :]) & earlier).astype(jnp.int32), axis=1)
    place = y_off * PAIR + position % LOCAL * MOST + rank
    target = jnp.zeros_like(z_off)
    for q, offset in enumerate(ORDER):
        inside = slot if offset in POOLED else place
        target = jnp.where(z_off == offset, START[q] + inside, target)
    code = jnp.broadcast_to((place + 1).astype(BF16)[None, :], (8, rows))

    chunk = 2 * NY * PAIR
    vmem = pl.BlockSpec(memory_space=pltpu.VMEM)
    hbm = pl.BlockSpec(memory_space=pl.ANY)
    dma = pltpu.SemaphoreType.DMA
    result = pl.pallas_call(
        kernel,
        out_shape=jax.ShapeDtypeStruct((rows, 2 * kv), BF16),
        in_specs=[vmem, vmem, vmem, vmem, hbm, hbm, hbm],
        out_specs=vmem,
        scratch_shapes=[
            pltpu.VMEM((rows, width), BF16),
            pltpu.VMEM((2, rows, width), BF16),
            pltpu.VMEM((2, 2 * width, kv), BF16),
            pltpu.VMEM((2 * width, kv), F32),
            pltpu.VMEM(adapter_down_maps.shape, BF16),
            pltpu.VMEM((LOCAL * 128, 2 * kv), BF16),
            pltpu.VMEM((rows, 2 * kv), F32),
            pltpu.VMEM((NZ, NY * PAIR, width), BF16),
            pltpu.VMEM((NZ, 8, 256), F32),
            pltpu.VMEM((NZ, NY * PAIR, width), BF16),
            pltpu.VMEM((NZ, 8, 256), F32),
            pltpu.VMEM((NZ, NY * PAIR, width), BF16),
            pltpu.VMEM((NZ, NY * PAIR, width), BF16),
            pltpu.VMEM((CHUNKS, NT, chunk // NT, 128), F32),
            pltpu.VMEM((CHUNKS, NT - 1, chunk // NT, 128), F32),
            pltpu.VMEM((CHUNKS, NT, chunk // NT, 128), BF16),
            pltpu.VMEM((NZ, NY * PAIR, 2 * kv), BF16),
            pltpu.VMEM((NZ, NY * PAIR, 2 * kv), BF16),
            pltpu.VMEM((NZ, NY * PAIR, 2 * kv), BF16),
            pltpu.VMEM((NZ, NY * PAIR, 2 * kv), BF16),
            dma, dma, dma((2,)), dma((2,)),
            dma((NZ,)), dma((NZ,)), dma((NZ,)), dma((NZ,)),
            dma((NZ, NY - 1)), dma((NZ, NY - 1)),
            dma((CHUNKS, NT - 1)), dma((CHUNKS, NT - 1)),
            dma((CHUNKS, NT - 1)), dma((CHUNKS, NT - 1)),
            dma((NZ, NY - 1)), dma((NZ, NY - 1)),
            dma((NZ,)), dma((NZ,)),
        ],
        compiler_params=pltpu.CompilerParams(
            collective_id=0, has_side_effects=True, vmem_limit_bytes=56 * 2**20
        ),
        cost_estimate=pl.CostEstimate(
            flops=12_000_000_000, bytes_accessed=24_000_000, transcendentals=0
        ),
    )(
        target[None, :], target[:, None], code,
        adapter_up_maps.reshape(LOCAL * 128, kv),
        tokens, key_value_weight.reshape(2 * full, kv), adapter_down_maps,
    )
    return result.reshape(rows, 2, kv)


def solution(mesh):
    in_specs = (
        P("req", None),
        P("req", None),
        P(),
        P(None, None, "tp"),
        P("req", "tp", None),
        P("req", None, None, "tp"),
    )
    out_specs = P("req", None, "tp")
    return jax.shard_map(local, mesh=mesh, in_specs=in_specs, out_specs=out_specs, check_vma=False)
```

time: 144 us -> 119 us (0.83); the launches traced: 141 us -> 119 us
  Pallas kernels: 133 us -> 110 us
    pallas_call x1, Pallas kernels: 133 us -> 110 us  [local(): pl.pallas_call(kernel, out_shape=jax.ShapeDtypeStruct((rows, 2 * kv), BF1...]
    select_n x0 -> x2, other arithmetic: none -> 3.28 us  [local(): target = jnp.where(z_off == offset, START[q] + inside, target)]
    add x2 -> x0, other arithmetic: 2.43 us -> none  [local(): target = turn * SLOTS + slot]
where the time goes in v2:
time: 119 us
  Pallas kernels  110 us (92%)
  other arithmetic  5.42 us (5%)
  local copies, waits for them, and re-layouts  3.23 us (3%)
    pallas_call x1, Pallas kernels, local(): pl.pallas_call(kernel, out_shape=jax.ShapeDtypeStruct((rows, 2 * kv), BF1...  110 us
    select_n x2, other arithmetic, local(): target = jnp.where(z_off == offset, START[q] + inside, target)  3.28 us

profile of v2, /device:TPU:32, one launch (start us, length us, event | category | flops | bytes accessed | tf_op | source)
XLA Modules:
  0.0 118.7 jit_solution(16490265234128728529)
XLA Ops:
  0.0 1.1 select_reduce_fusion
  1.1 0.5 convert_reduce_fusion.1
  1.6 0.5 convert_reduce_fusion
  2.2 0.7 compare_select_fusion.11.tgt_row
  2.9 0.2 copy.20
  3.1 0.2 copy.19
  3.3 0.2 copy.15
  3.6 2.6 %select_select_fusion.tgt_col = s32[1024,1]{1,0:T(8,128)} fusion(s32[1024,1]{1,0:T(8,128)S(1)} %copy.20, s32[1024,1]{1,0:T(8,128)S(1)} %copy.19, s32[1024,1]{1,0:T(8,128)S(1)} %copy.15, s32[]{:T(128)S(6)} %select_n.337, s32[]{:T(128)S(6)} %select_n.334), kind=kLoop, calls=%fused_computation.33 | loop fusion | flops 93184 | bytes 16392 | tf_op jit(solution)/shard_map/jit(_where)/select_n | solution.py:372
  6.1 0.6 broadcast_in_dim.16.code
  6.7 109.9 %shard_map.64 = bf16[1024,256]{1,0:T(8,128)(2,1)} custom-call(s32[1,1024]{1,0:T(1,128)} %compare_select_fusion.11.tgt_row, s32[1024,1]{1,0:T(8,128)} %select_select_fusion.tgt_col, bf16[8,1024]{1,0:T(8,128)(2,1)} %broadcast_in_dim.16.code, bf16[1024,128]{1,0:T(8,128)(2,1)} %bitcast.17, bf16[1024,8192]{1,0:T(8,128)(2,1)} %tokens.1, ...), custom_call_target="tpu_custom_call" | custom-call | flops 12000000000 | bytes 24000000 | tf_op jit(solution)/shard_map/pallas_call | solution.py:379
  116.7 2.0 %reshape.622 = bf16[1024,2,128]{2,1,0:T(2,128)(2,1)} reshape(bf16[1024,256]{1,0:T(8,128)(2,1)} %shard_map.64) | data formatting | bytes 1048576 | tf_op jit(solution)/shard_map/reshape | solution.py:424
  (1 shorter events, 0.0 us)

commit v3 on v2

--- a/solution.py
+++ b/solution.py
@@ -25,8 +25,8 @@
 
 
 def kernel(
-    tgt_row, tgt_col, code, up, tokens, weight, down, out,
-    x, tok, wbuf, w32, amaps, umat, acc,
+    tgt_row, code, up, tokens, weight, down, out,
+    x, tok, wbuf, w32, amaps, umat, acc, tgt_col, picks,
     packed, meta_out, mid, meta_in, yout, yin, part, rs_in, gath, dout, rmid, zret, fin,
     x_sem, a_sem, tok_sem, w_sem,
     z_ss, z_rs, m_ss, m_rs, y_ss, y_rs, r_ss, r_rs, g_ss, g_rs, yr_ss, yr_rs, zr_ss, zr_rs,
@@ -94,10 +94,13 @@
         pooled = [i for i in range(2) if ORDER[2 * k + i] in POOLED]
         if pooled:
             codes = lax.dot_general(
-                code[...], pick, (((1,), (1,)), ((), ())), preferred_element_type=F32
+                jnp.broadcast_to(code[...], (8, rows)).astype(BF16), pick,
+                (((1,), (1,)), ((), ())), preferred_element_type=F32,
             )
         for i in pooled:
             meta_out[2 * k + i, :, 0:SLOTS] = codes[:, begin[i] : begin[i] + SLOTS]
+        if k == 0:
+            x_copy.wait()
         for n in range(width // 256):
             cols = slice(n * 256, (n + 1) * 256)
             block = dot(pick, x[:, cols]).astype(BF16)
@@ -107,6 +110,8 @@
                 if i not in pooled:
                     land = yin if ORDER[q] == 0 else mid
                     land[q, 0:PAIR, cols] = block[begin[i] : begin[i] + PAIR]
+        if k == 0:
+            pl.semaphore_wait(barrier, len(peers))
         for i in range(2):
             q = 2 * k + i
             if i in pooled:
@@ -257,13 +262,12 @@
             for d in range(1, NY):
                 yr_copies[q, d].wait_recv()
 
+        count = SIZE[2 * k] + SIZE[2 * k + 1]
+        rows_in = jnp.concatenate([fin[q, 0 : SIZE[q]] for q in (2 * k, 2 * k + 1)], axis=0)
+
         def body(r, carry):
             span = pl.ds(pl.multiple_of(r * tile, tile), tile)
-            total = acc[span, :]
-            for q in (2 * k, 2 * k + 1):
-                slot_id = lax.broadcasted_iota(jnp.int32, (tile, SIZE[q]), 1) + START[q]
-                pick = jnp.where(slot_id == tgt_col[span, :], 1.0, 0.0).astype(BF16)
-                total = total + dot(pick, fin[q, 0 : SIZE[q]])
+            total = acc[span, :] + dot(picks[k, span, 0:count], rows_in)
             if last:
                 out[span, :] = total.astype(BF16)
             else:
@@ -272,6 +276,17 @@
 
         lax.fori_loop(0, rows // tile, body, 0)
 
+    def choose(k):
+        count = SIZE[2 * k] + SIZE[2 * k + 1]
+
+        def body(r, carry):
+            span = pl.ds(pl.multiple_of(r * tile, tile), tile)
+            slot_id = (lax.broadcasted_iota(jnp.int32, (tile, count), 1) + START[2 * k]).astype(F32)
+            picks[k, span, 0:count] = jnp.where(slot_id == tgt_col[span, 0:1], 1.0, 0.0).astype(BF16)
+            return carry
+
+        lax.fori_loop(0, rows // tile, body, 0)
+
     def base(first, stop):
         def step(s, carry):
             slot = lax.rem(s, 2)
@@ -298,32 +313,34 @@
 
         lax.fori_loop(first, stop, step, 0)
 
+    pack(0)
+    a_copy.start()
+    for copy in base_copies(0, 0):
+        copy.start()
+    pack(1)
+    pack(2)
+    pack(3)
     rank_row = lax.broadcasted_iota(jnp.int32, up.shape, 0) % 128
     umat[:, 0:128] = jnp.where(rank_row < 64, up[...].astype(F32), 0.0).astype(BF16)
     umat[:, 128:256] = jnp.where(rank_row < 64, 0.0, up[...].astype(F32)).astype(BF16)
-
-    x_copy.wait()
-    a_copy.start()
-    for copy in base_copies(0, 0):
-        copy.start()
     acc[...] = jnp.zeros_like(acc)
-    pl.semaphore_wait(barrier, len(peers))
-    pack(0)
-    pack(1)
-    pack(2)
-    pack(3)
-    base(0, 4)
+    tgt_col[...] = jnp.transpose(jnp.broadcast_to(tgt_row[...].astype(F32), (8, rows)))
+    base(0, 5)
+    choose(0)
+    choose(1)
     a_copy.wait()
     repack(0)
     forward(2)
     project(0)
     forward(3)
     reduce(0)
-    base(4, 6)
+    base(5, 7)
     expand(0)
-    base(6, 8)
+    base(7, 8)
     unpack(0)
     repack(1)
+    choose(2)
+    choose(3)
     project(1)
     reduce(1)
     expand(1)
@@ -370,7 +387,7 @@
     for q, offset in enumerate(ORDER):
         inside = slot if offset in POOLED else place
         target = jnp.where(z_off == offset, START[q] + inside, target)
-    code = jnp.broadcast_to((place + 1).astype(BF16)[None, :], (8, rows))
+    code = (place + 1).astype(F32)
 
     chunk = 2 * NY * PAIR
     vmem = pl.BlockSpec(memory_space=pltpu.VMEM)
@@ -379,7 +396,7 @@
     result = pl.pallas_call(
         kernel,
         out_shape=jax.ShapeDtypeStruct((rows, 2 * kv), BF16),
-        in_specs=[vmem, vmem, vmem, vmem, hbm, hbm, hbm],
+        in_specs=[vmem, vmem, vmem, hbm, hbm, hbm],
         out_specs=vmem,
         scratch_shapes=[
             pltpu.VMEM((rows, width), BF16),
@@ -389,6 +406,8 @@
             pltpu.VMEM(adapter_down_maps.shape, BF16),
             pltpu.VMEM((LOCAL * 128, 2 * kv), BF16),
             pltpu.VMEM((rows, 2 * kv), F32),
+            pltpu.VMEM((rows, 8), F32),
+            pltpu.VMEM((CHUNKS, rows, 2 * NY * PAIR), BF16),
             pltpu.VMEM((NZ, NY * PAIR, width), BF16),
             pltpu.VMEM((NZ, 8, 256), F32),
             pltpu.VMEM((NZ, NY * PAIR, width), BF16),
@@ -417,7 +436,7 @@
             flops=12_000_000_000, bytes_accessed=24_000_000, transcendentals=0
         ),
     )(
-        target[None, :], target[:, None], code,
+        target[None, :], code[None, :],
         adapter_up_maps.reshape(LOCAL * 128, kv),
         tokens, key_value_weight.reshape(2 * full, kv), adapter_down_maps,
     )

time: 119 us -> 114 us (0.958)
  Pallas kernels: 110 us -> 108 us
  other arithmetic: 5.42 us -> 3.46 us
  local copies, waits for them, and re-layouts: 3.23 us -> 1.96 us
    select_n x2 -> x1, other arithmetic: 3.28 us -> 0.65 us  [local(): target = jnp.where(z_off == offset, START[q] + inside, target)]
    pallas_call x1, Pallas kernels: 110 us -> 108 us  [local(): pl.pallas_call(kernel, out_shape=jax.ShapeDtypeStruct((rows, 2 * kv), BF1...]
where the time goes in v3:
time: 114 us
  Pallas kernels  108 us (95%)
  other arithmetic  3.46 us (3%)
  local copies, waits for them, and re-layouts  1.96 us (2%)
    pallas_call x1, Pallas kernels, local(): pl.pallas_call(kernel, out_shape=jax.ShapeDtypeStruct((rows, 2 * kv), BF1...  108 us

profile of v3, /device:TPU:32, one launch (start us, length us, event | category | flops | bytes accessed | tf_op | source)
XLA Modules:
  0.0 113.6 jit_solution(8757960276553921833)
XLA Ops:
  0.0 1.1 select_reduce_fusion
  1.1 0.5 convert_reduce_fusion.1
  1.6 0.5 convert_reduce_fusion
  2.1 0.7 add_convert_fusion
  2.8 0.6 compare_select_fusion.11.tgt_row
  3.5 108.2 %shard_map.64 = bf16[1024,256]{1,0:T(8,128)(2,1)} custom-call(s32[1,1024]{1,0:T(1,128)} %compare_select_fusion.11.tgt_row, f32[1,1024]{1,0:T(1,128)} %get-tuple-element.5.code, bf16[1024,128]{1,0:T(8,128)(2,1)} %bitcast.11, bf16[1024,8192]{1,0:T(8,128)(2,1)} %tokens.1, bf16[16384,128]{1,0:T(8,128)(2,1)} %bitcast.10, bf16[8,1024,128]{2,1,0:T(8,128)(2,1)} %down.1), custom_call_target="tpu_custom_call" | custom-call | flops 12000000000 | bytes 24000000 | tf_op jit(solution)/shard_map/pallas_call | solution.py:396
  111.7 2.0 %reshape.370 = bf16[1024,2,128]{2,1,0:T(2,128)(2,1)} reshape(bf16[1024,256]{1,0:T(8,128)(2,1)} %shard_map.64) | data formatting | bytes 1048576 | tf_op jit(solution)/shard_map/reshape | solution.py:443
  (1 shorter events, 0.0 us)

commit v4 on v3

--- a/solution.py
+++ b/solution.py
@@ -14,7 +14,7 @@
 LOCAL, MOST = 8, 6
 PAIR = LOCAL * MOST
 POOLED = (4, 3, 5)
-SLOTS = 192
+SLOTS = 160
 SIZE = tuple(SLOTS if d in POOLED else NY * PAIR for d in ORDER)
 START = tuple(sum(SIZE[:q]) for q in range(NZ))
 BF16, F32 = jnp.bfloat16, jnp.float32
@@ -25,11 +25,11 @@
 
 
 def kernel(
-    tgt_row, code, up, tokens, weight, down, out,
+    tgt_row, code, up, tokens, weight, down, out, over,
     x, tok, wbuf, w32, amaps, umat, acc, tgt_col, picks,
-    packed, meta_out, mid, meta_in, yout, yin, part, rs_in, gath, dout, rmid, zret, fin,
+    packed, meta_out, mid, meta_in, yout, yin, part, rs_in, gath, dout, rmid, zret, fin, flags,
     x_sem, a_sem, tok_sem, w_sem,
-    z_ss, z_rs, m_ss, m_rs, y_ss, y_rs, r_ss, r_rs, g_ss, g_rs, yr_ss, yr_rs, zr_ss, zr_rs,
+    z_ss, z_rs, m_ss, m_rs, y_ss, y_rs, r_ss, r_rs, g_ss, g_rs, yr_ss, yr_rs, zr_ss, zr_rs, f_ss, f_rs,
 ):
     group = lax.axis_index("req")
     t = lax.axis_index("tp")
@@ -74,7 +74,9 @@
         )
 
     sent = []
-    m_copies, z_copies, y_copies, r_copies, g_copies, yr_copies, zr_copies = ({} for _ in range(7))
+    m_copies, z_copies, y_copies, r_copies, g_copies, yr_copies, zr_copies, f_copies = (
+        {} for _ in range(8)
+    )
 
     def half(d):
         return pl.ds(d * PAIR, PAIR)
@@ -314,6 +316,12 @@
         lax.fori_loop(first, stop, step, 0)
 
     pack(0)
+    dropped = jnp.where(tgt_row[...] < 0, 1.0, 0.0)
+    flags[0] = jnp.broadcast_to(jnp.max(dropped, axis=1, keepdims=True), flags.shape[1:])
+    for d in range(1, NZ):
+        send(f_copies, d, remote(
+            flags.at[0], flags.at[d], f_ss.at[d - 1], f_rs.at[d - 1], at_yz(0, d)
+        ))
     a_copy.start()
     for copy in base_copies(0, 0):
         copy.start()
@@ -326,6 +334,13 @@
     acc[...] = jnp.zeros_like(acc)
     tgt_col[...] = jnp.transpose(jnp.broadcast_to(tgt_row[...].astype(F32), (8, rows)))
     base(0, 5)
+    for d in range(1, NZ):
+        f_copies[d].wait_recv()
+    flags[NZ] = jnp.max(flags[0:NZ], axis=0)
+    for d in range(1, NY):
+        send(f_copies, NZ + d, remote(
+            flags.at[NZ], flags.at[NZ + d], f_ss.at[NZ + d - 2], f_rs.at[NZ + d - 2], at_yz(d, 0)
+        ))
     choose(0)
     choose(1)
     a_copy.wait()
@@ -357,8 +372,42 @@
     back(3)
     collect(2, False)
     collect(3, True)
+    for d in range(1, NY):
+        f_copies[NZ + d].wait_recv()
+    over[...] = jnp.max(flags[NZ : NZ + NY], axis=0)
     for copy in sent:
         copy.wait_send()
+
+
+def general(tokens, position, key_value_weight, adapter_down_maps, adapter_up_maps):
+    rows, full = tokens.shape
+    groups = NY * NZ
+    width, rank = adapter_down_maps.shape[1:]
+    kv = key_value_weight.shape[2]
+    seq = jnp.arange(rows, dtype=jnp.int32)
+    earlier = (position[:, None] == position[None, :]) & (seq[None, :] < seq[:, None])
+    place = jnp.sum(earlier.astype(jnp.int32), axis=1)
+    target = position // LOCAL * PAIR + position % LOCAL * MOST + place
+    own = lax.dynamic_slice_in_dim(tokens, lax.axis_index("tp") * width, width, 1)
+    outgoing = jnp.zeros((groups * PAIR, width), BF16).at[target].set(own)
+    arrived = lax.all_to_all(
+        outgoing.reshape(groups, PAIR, width), "req", split_axis=0, concat_axis=0, tiled=True
+    )
+    partial = jnp.einsum(
+        "uebf,efn->uebn", arrived.reshape(groups, LOCAL, MOST, width), adapter_down_maps,
+        preferred_element_type=F32,
+    )
+    shrunk = lax.psum(partial, "tp").astype(BF16)
+    delta = jnp.einsum(
+        "fipst,istk->fipsk", shrunk.reshape(groups, LOCAL, MOST, 2, rank // 2), adapter_up_maps,
+        preferred_element_type=F32,
+    ).astype(BF16)
+    returned = lax.all_to_all(
+        delta.reshape(groups, PAIR, 2, kv), "req", split_axis=0, concat_axis=0, tiled=True
+    )
+    own_delta = returned.reshape(groups * PAIR, 2, kv)[target]
+    base = dot(tokens, key_value_weight.reshape(full, 2 * kv)).reshape(rows, 2, kv)
+    return (base + own_delta.astype(F32)).astype(BF16)
 
 
 def local(
@@ -385,19 +434,24 @@
     place = y_off * PAIR + position % LOCAL * MOST + rank
     target = jnp.zeros_like(z_off)
     for q, offset in enumerate(ORDER):
-        inside = slot if offset in POOLED else place
-        target = jnp.where(z_off == offset, START[q] + inside, target)
+        inside = START[q] + place
+        if offset in POOLED:
+            inside = jnp.where(slot < SLOTS, START[q] + slot, -1)
+        target = jnp.where(z_off == offset, inside, target)
     code = (place + 1).astype(F32)
 
     chunk = 2 * NY * PAIR
     vmem = pl.BlockSpec(memory_space=pltpu.VMEM)
     hbm = pl.BlockSpec(memory_space=pl.ANY)
     dma = pltpu.SemaphoreType.DMA
-    result = pl.pallas_call(
+    result, over = pl.pallas_call(
         kernel,
-        out_shape=jax.ShapeDtypeStruct((rows, 2 * kv), BF16),
+        out_shape=(
+            jax.ShapeDtypeStruct((rows, 2 * kv), BF16),
+            jax.ShapeDtypeStruct((8, 128), F32),
+        ),
         in_specs=[vmem, vmem, vmem, hbm, hbm, hbm],
-        out_specs=vmem,
+        out_specs=(vmem, vmem),
         scratch_shapes=[
             pltpu.VMEM((rows, width), BF16),
             pltpu.VMEM((2, rows, width), BF16),
@@ -421,6 +475,7 @@
             pltpu.VMEM((NZ, NY * PAIR, 2 * kv), BF16),
             pltpu.VMEM((NZ, NY * PAIR, 2 * kv), BF16),
             pltpu.VMEM((NZ, NY * PAIR, 2 * kv), BF16),
+            pltpu.VMEM((NZ + NY, 8, 128), F32),
             dma, dma, dma((2,)), dma((2,)),
             dma((NZ,)), dma((NZ,)), dma((NZ,)), dma((NZ,)),
             dma((NZ, NY - 1)), dma((NZ, NY - 1)),
@@ -428,6 +483,7 @@
             dma((CHUNKS, NT - 1)), dma((CHUNKS, NT - 1)),
             dma((NZ, NY - 1)), dma((NZ, NY - 1)),
             dma((NZ,)), dma((NZ,)),
+            dma((NZ + NY - 2,)), dma((NZ + NY - 2,)),
         ],
         compiler_params=pltpu.CompilerParams(
             collective_id=0, has_side_effects=True, vmem_limit_bytes=56 * 2**20
@@ -440,7 +496,12 @@
         adapter_up_maps.reshape(LOCAL * 128, kv),
         tokens, key_value_weight.reshape(2 * full, kv), adapter_down_maps,
     )
-    return result.reshape(rows, 2, kv)
+    args = (
+        tokens, position, key_value_weight, adapter_down_maps, adapter_up_maps,
+    )
+    return lax.cond(
+        over[0, 0] > 0, lambda: general(*args), lambda: result.reshape(rows, 2, kv)
+    )
 
 
 def solution(mesh):

time: 114 us -> 109 us (0.956)
  Pallas kernels: 108 us -> 102 us
    pallas_call x1, Pallas kernels: 108 us -> 102 us  [local(): pl.pallas_call(kernel, out_shape=(jax.ShapeDtypeStruct((rows, 2 * kv), BF...]
    reshape x1 -> x0, local copies, waits for them, and re-layouts: 1.96 us -> none  [local(): return result.reshape(rows, 2, kv)]
    slice x0 -> x1, local copies, waits for them, and re-layouts: none -> 1.18 us  [local(): over[0, 0] > 0]
where the time goes in v4:
time: 109 us
  Pallas kernels  102 us (94%)
  other arithmetic  3.46 us (3%)
  local copies, waits for them, and re-layouts  2.59 us (2%)
    pallas_call x1, Pallas kernels, local(): pl.pallas_call(kernel, out_shape=(jax.ShapeDtypeStruct((rows, 2 * kv), BF...  102 us

profile of v4, /device:TPU:32, one launch (start us, length us, event | category | flops | bytes accessed | tf_op | source)
XLA Modules:
  0.0 108.6 jit_solution(14178170405308279984)
XLA Ops:
  0.0 1.1 select_reduce_fusion
  1.1 0.5 convert_reduce_fusion.1
  1.6 0.5 convert_reduce_fusion.2
  2.1 0.7 add_convert_fusion
  2.8 0.7 compare_select_fusion.12.tgt_row
  3.5 0.0 copy-start.2
  3.5 101.6 %shard_map.66 = (bf16[1024,256]{1,0:T(8,128)(2,1)S(1)}, f32[8,128]{1,0:T(8,128)}) custom-call(s32[1,1024]{1,0:T(1,128)} %compare_select_fusion.12.tgt_row, f32[1,1024]{1,0:T(1,128)} %get-tuple-element.55.code, bf16[1024,128]{1,0:T(8,128)(2,1)} %bitcast.58, bf16[1024,8192]{1,0:T(8,128)(2,1)} %tokens.1, bf16[16384,128]{1,0:T(8,128)(2,1)} %bitcast.54, ...), custom_call_target="tpu_custom_call" | custom-call | flops 12000000000 | bytes 24000000 | tf_op jit(solution)/shard_map/pallas_call | solution.py:447
  105.1 1.2 %slice.3 = f32[1,1]{1,0:T(1,128)} slice(f32[8,128]{1,0:T(8,128)} %get-tuple-element.26), slice={[0:1], [0:1]} | slice | bytes 8 | tf_op jit(solution)/shard_map/slice | solution.py:503
  106.9 0.0 copy-done.2
  106.9 0.9 conditional.1
  106.9 0.2 copy.36
  107.1 0.4 copy.41
  107.8 0.0 copy-start.1
  107.8 0.8 copy-done.1
  (1 shorter events, 0.0 us)
Async XLA Ops:
  3.5 103.4 %copy-start.2 = (bf16[8,2,64,128]{3,2,1,0:T(8,128)(2,1)S(1)}, bf16[8,2,64,128]{3,2,1,0:T(8,128)(2,1)}, u32[]{:S(2)}) copy-start(bf16[8,2,64,128]{3,2,1,0:T(8,128)(2,1)} %param.13) | copy-start | bytes 786436
  107.8 0.8 copy-start.1

commit v5 on v4

--- a/solution.py
+++ b/solution.py
@@ -25,8 +25,8 @@
 
 
 def kernel(
-    tgt_row, code, up, tokens, weight, down, out, over,
-    x, tok, wbuf, w32, amaps, umat, acc, tgt_col, picks,
+    chosen, store, up, tokens, weight, down, out, over,
+    x, tok, wbuf, w32, amaps, umat, acc, tgt_row, code, tgt_col, picks,
     packed, meta_out, mid, meta_in, yout, yin, part, rs_in, gath, dout, rmid, zret, fin, flags,
     x_sem, a_sem, tok_sem, w_sem,
     z_ss, z_rs, m_ss, m_rs, y_ss, y_rs, r_ss, r_rs, g_ss, g_rs, yr_ss, yr_rs, zr_ss, zr_rs, f_ss, f_rs,
@@ -55,6 +55,44 @@
     )
     x_copy.start()
     a_copy = pltpu.make_async_copy(down, amaps, a_sem)
+
+    def column(row):
+        return jnp.transpose(jnp.broadcast_to(row, (8, row.shape[1])))[:, 0:1]
+
+    def assign():
+        adapters = store.shape[1]
+        table = lax.broadcasted_iota(jnp.int32, (adapters, rows), 0)
+        found = jnp.where(table == chosen[...], column(store[...].astype(F32)), 0.0)
+        position = jnp.sum(found, axis=0, keepdims=True)
+        position_col = column(position)
+        place = position.astype(jnp.int32)
+        owner, adapter = place >> 3, place & (LOCAL - 1)
+        y_off = (owner // NZ - y + NY) & (NY - 1)
+        z_to = owner & (NZ - 1)
+        z_off = (z_to - z + NZ) & (NZ - 1)
+        total = jnp.zeros((1, rows), F32)
+        for r in range(rows // 256):
+            other = position_col[r * 256 : (r + 1) * 256]
+            other_z = (other.astype(jnp.int32) >> 3) & (NZ - 1)
+            shape = (256, rows)
+            earlier = (
+                lax.broadcasted_iota(jnp.int32, shape, 0) + r * 256
+                < lax.broadcasted_iota(jnp.int32, shape, 1)
+            )
+            weight_of = jnp.where(other == position, 2049.0, 1.0)
+            counted = jnp.where(earlier & (other_z == z_to), weight_of, 0.0)
+            total = total + jnp.sum(counted, axis=0, keepdims=True)
+        both = total.astype(jnp.int32)
+        rank, slot = both >> 11, both & 2047
+        inside = y_off * PAIR + adapter * MOST + rank
+        target = jnp.zeros_like(slot)
+        for q, offset in enumerate(ORDER):
+            here = START[q] + inside
+            if offset in POOLED:
+                here = jnp.where(slot < SLOTS, START[q] + slot, -1)
+            target = jnp.where(z_off == offset, here, target)
+        tgt_row[...] = target
+        code[...] = (inside + 1).astype(F32)
 
     def base_copies(step, slot):
         return (
@@ -315,6 +353,7 @@
 
         lax.fori_loop(first, stop, step, 0)
 
+    assign()
     pack(0)
     dropped = jnp.where(tgt_row[...] < 0, 1.0, 0.0)
     flags[0] = jnp.broadcast_to(jnp.max(dropped, axis=1, keepdims=True), flags.shape[1:])
@@ -358,32 +397,38 @@
     choose(3)
     project(1)
     reduce(1)
+    project(2)
     expand(1)
-    project(2)
-    unpack(1)
     reduce(2)
     project(3)
+    unpack(1)
     expand(2)
     collect(0, False)
     reduce(3)
+    collect(1, False)
+    expand(3)
     back(2)
-    expand(3)
-    collect(1, False)
     back(3)
     collect(2, False)
     collect(3, True)
     for d in range(1, NY):
         f_copies[NZ + d].wait_recv()
-    over[...] = jnp.max(flags[NZ : NZ + NY], axis=0)
+    over[0, 0] = jnp.max(flags[NZ : NZ + NY])
     for copy in sent:
         copy.wait_send()
 
 
-def general(tokens, position, key_value_weight, adapter_down_maps, adapter_up_maps):
+def general(
+    tokens, request_adapter, storage_position, key_value_weight, adapter_down_maps, adapter_up_maps
+):
     rows, full = tokens.shape
     groups = NY * NZ
     width, rank = adapter_down_maps.shape[1:]
     kv = key_value_weight.shape[2]
+    table = jnp.arange(storage_position.shape[0], dtype=jnp.int32)
+    position = jnp.sum(
+        jnp.where(request_adapter == table[None, :], storage_position[None, :], 0), axis=1
+    )
     seq = jnp.arange(rows, dtype=jnp.int32)
     earlier = (position[:, None] == position[None, :]) & (seq[None, :] < seq[:, None])
     place = jnp.sum(earlier.astype(jnp.int32), axis=1)
@@ -417,29 +462,6 @@
     width = adapter_down_maps.shape[1]
     kv = key_value_weight.shape[2]
     adapters = storage_position.shape[0]
-    group = lax.axis_index("req")
-    y, z = group // NZ, group % NZ
-    chosen = request_adapter[:, 0]
-    table = jnp.arange(adapters, dtype=jnp.int32)
-    position = jnp.sum(
-        jnp.where(chosen[:, None] == table[None, :], storage_position[None, :], 0), axis=1
-    )
-    owner = position // LOCAL
-    y_off = (owner // NZ - y + NY) % NY
-    z_off = (owner % NZ - z + NZ) % NZ
-    seq = jnp.arange(rows, dtype=jnp.int32)
-    earlier = seq[None, :] < seq[:, None]
-    rank = jnp.sum(((position[:, None] == position[None, :]) & earlier).astype(jnp.int32), axis=1)
-    slot = jnp.sum(((z_off[:, None] == z_off[None, :]) & earlier).astype(jnp.int32), axis=1)
-    place = y_off * PAIR + position % LOCAL * MOST + rank
-    target = jnp.zeros_like(z_off)
-    for q, offset in enumerate(ORDER):
-        inside = START[q] + place
-        if offset in POOLED:
-            inside = jnp.where(slot < SLOTS, START[q] + slot, -1)
-        target = jnp.where(z_off == offset, inside, target)
-    code = (place + 1).astype(F32)
-
     chunk = 2 * NY * PAIR
     vmem = pl.BlockSpec(memory_space=pltpu.VMEM)
     hbm = pl.BlockSpec(memory_space=pl.ANY)
@@ -448,10 +470,10 @@
         kernel,
         out_shape=(
             jax.ShapeDtypeStruct((rows, 2 * kv), BF16),
-            jax.ShapeDtypeStruct((8, 128), F32),
+            jax.ShapeDtypeStruct((1, 1), F32),
         ),
         in_specs=[vmem, vmem, vmem, hbm, hbm, hbm],
-        out_specs=(vmem, vmem),
+        out_specs=(vmem, pl.BlockSpec(memory_space=pltpu.SMEM)),
         scratch_shapes=[
             pltpu.VMEM((rows, width), BF16),
             pltpu.VMEM((2, rows, width), BF16),
@@ -460,6 +482,8 @@
             pltpu.VMEM(adapter_down_maps.shape, BF16),
             pltpu.VMEM((LOCAL * 128, 2 * kv), BF16),
             pltpu.VMEM((rows, 2 * kv), F32),
+            pltpu.VMEM((1, rows), jnp.int32),
+            pltpu.VMEM((1, rows), F32),
             pltpu.VMEM((rows, 8), F32),
             pltpu.VMEM((CHUNKS, rows, 2 * NY * PAIR), BF16),
             pltpu.VMEM((NZ, NY * PAIR, width), BF16),
@@ -492,12 +516,13 @@
             flops=12_000_000_000, bytes_accessed=24_000_000, transcendentals=0
         ),
     )(
-        target[None, :], code[None, :],
+        request_adapter.reshape(1, rows), storage_position.reshape(1, adapters),
         adapter_up_maps.reshape(LOCAL * 128, kv),
         tokens, key_value_weight.reshape(2 * full, kv), adapter_down_maps,
     )
     args = (
-        tokens, position, key_value_weight, adapter_down_maps, adapter_up_maps,
+        tokens, request_adapter, storage_position, key_value_weight, adapter_down_maps,
+        adapter_up_maps,
     )
     return lax.cond(
         over[0, 0] > 0, lambda: general(*args), lambda: result.reshape(rows, 2, kv)

time: 109 us -> 103 us (0.945)
  other arithmetic: 3.46 us -> 0 us
  Pallas kernels: 102 us -> 99.4 us
  local copies, waits for them, and re-layouts: 2.59 us -> 1.42 us
    pallas_call x1, Pallas kernels: 102 us -> 99.4 us  [local(): pl.pallas_call(kernel, out_shape=(jax.ShapeDtypeStruct((rows, 2 * kv), BF...]
    reduce_sum x3 -> x0, other arithmetic: 2.11 us -> none  [the longest x1 1.06 us: local(): jnp.sum(jnp.where(chosen[:, None] == table[None, :], storage_position[Non...]
    slice x1 -> x0, local copies, waits for them, and re-layouts: 1.18 us -> none  [local(): over[0, 0] > 0]
where the time goes in v5:
time: 103 us; the launch traced here: 102 us
  Pallas kernels  99.4 us (97%)
  local copies, waits for them, and re-layouts  1.42 us (1%)
    pallas_call x1, Pallas kernels, local(): pl.pallas_call(kernel, out_shape=(jax.ShapeDtypeStruct((rows, 2 * kv), BF...  99.4 us

profile of v5, /device:TPU:32, one launch (start us, length us, event | category | flops | bytes accessed | tf_op | source)
XLA Modules:
  0.0 101.8 jit_solution(3541710319634219825)
XLA Ops:
  0.0 0.0 copy-start.2
  0.0 0.0 copy-start.3
  0.0 0.0 copy-start.4
  0.0 99.4 %shard_map.66 = (bf16[1024,256]{1,0:T(8,128)(2,1)S(1)}, f32[1,1]{1,0:T(1,128)}) custom-call(s32[1,1024]{1,0:T(1,128)} %bitcast.65, s32[1,256]{1,0:T(1,128)} %bitcast.67, bf16[1024,128]{1,0:T(8,128)(2,1)} %bitcast.60, bf16[1024,8192]{1,0:T(8,128)(2,1)} %tokens.1, bf16[16384,128]{1,0:T(8,128)(2,1)} %bitcast.56, bf16[8,1024,128]{2,1,0:T(8,128)(2,1)} %down.1), custom_call_target="tpu_custom_call" | custom-call | flops 12000000000 | bytes 24000000 | tf_op jit(solution)/shard_map/pallas_call | solution.py:469
  100.1 0.0 copy-done.2
  100.1 0.0 copy-done.3
  100.1 0.0 copy-done.4
  100.2 0.9 conditional.1
  100.2 0.2 copy.36
  100.4 0.4 copy.41
  101.0 0.0 copy-start.1
  101.0 0.8 copy-done.1
Async XLA Ops:
  0.0 100.1 %copy-start.2 = (bf16[8,2,64,128]{3,2,1,0:T(8,128)(2,1)S(1)}, bf16[8,2,64,128]{3,2,1,0:T(8,128)(2,1)}, u32[]{:S(2)}) copy-start(bf16[8,2,64,128]{3,2,1,0:T(8,128)(2,1)} %param.13) | copy-start | bytes 786436
  0.0 100.1 %copy-start.3 = (s32[1024,1]{0,1:T(1,128)S(1)}, s32[1024,1]{0,1:T(1,128)}, u32[]{:S(2)}) copy-start(s32[1024,1]{0,1:T(1,128)} %param.9) | copy-start | bytes 12292
  0.0 100.1 %copy-start.4 = (s32[256]{0:T(256)S(1)}, s32[256]{0:T(256)}, u32[]{:S(2)}) copy-start(s32[256]{0:T(256)} %param.10) | copy-start | bytes 3076
  101.0 0.8 copy-start.1

commit v6 on v5

--- a/solution.py
+++ b/solution.py
@@ -70,18 +70,24 @@
         y_off = (owner // NZ - y + NY) & (NY - 1)
         z_to = owner & (NZ - 1)
         z_off = (z_to - z + NZ) & (NZ - 1)
-        total = jnp.zeros((1, rows), F32)
-        for r in range(rows // 256):
-            other = position_col[r * 256 : (r + 1) * 256]
-            other_z = (other.astype(jnp.int32) >> 3) & (NZ - 1)
-            shape = (256, rows)
-            earlier = (
-                lax.broadcasted_iota(jnp.int32, shape, 0) + r * 256
-                < lax.broadcasted_iota(jnp.int32, shape, 1)
-            )
-            weight_of = jnp.where(other == position, 2049.0, 1.0)
-            counted = jnp.where(earlier & (other_z == z_to), weight_of, 0.0)
-            total = total + jnp.sum(counted, axis=0, keepdims=True)
+        side = 256
+        spans = [slice(r * side, (r + 1) * side) for r in range(rows // side)]
+        other = [position_col[span] for span in spans]
+        other_z = [(o.astype(jnp.int32) >> 3) & (NZ - 1) for o in other]
+        before = lax.broadcasted_iota(jnp.int32, (side, side), 0) < lax.broadcasted_iota(
+            jnp.int32, (side, side), 1
+        )
+        totals = []
+        for j, span in enumerate(spans):
+            total = jnp.zeros((1, side), F32)
+            for r in range(j + 1):
+                counted = jnp.where(other[r] == position[:, span], 2049.0, 1.0)
+                counted = jnp.where(other_z[r] == z_to[:, span], counted, 0.0)
+                if r == j:
+                    counted = jnp.where(before, counted, 0.0)
+                total = total + jnp.sum(counted, axis=0, keepdims=True)
+            totals.append(total)
+        total = jnp.concatenate(totals, axis=1)
         both = total.astype(jnp.int32)
         rank, slot = both >> 11, both & 2047
         inside = y_off * PAIR + adapter * MOST + rank
@@ -126,39 +132,29 @@
 
     span = pl.ds(0, SLOTS)
 
-    def pack(k):
-        count = SIZE[2 * k] + SIZE[2 * k + 1]
-        slot_id = lax.broadcasted_iota(jnp.int32, (count, rows), 0) + START[2 * k]
+    def pack(*turns):
+        count = sum(SIZE[q] for q in turns)
+        slot_id = lax.broadcasted_iota(jnp.int32, (count, rows), 0) + START[turns[0]]
         pick = jnp.where(slot_id == tgt_row[...], 1.0, 0.0).astype(BF16)
-        begin = (0, SIZE[2 * k])
-        pooled = [i for i in range(2) if ORDER[2 * k + i] in POOLED]
-        if pooled:
-            codes = lax.dot_general(
-                jnp.broadcast_to(code[...], (8, rows)).astype(BF16), pick,
-                (((1,), (1,)), ((), ())), preferred_element_type=F32,
-            )
-        for i in pooled:
-            meta_out[2 * k + i, :, 0:SLOTS] = codes[:, begin[i] : begin[i] + SLOTS]
-        if k == 0:
+        first = 0 in turns
+        if first:
             x_copy.wait()
         for n in range(width // 256):
             cols = slice(n * 256, (n + 1) * 256)
             block = dot(pick, x[:, cols]).astype(BF16)
-            for i in range(2):
-                q = 2 * k + i
-                packed[q, 0 : SIZE[q], cols] = block[begin[i] : begin[i] + SIZE[q]]
-                if i not in pooled:
+            for q in turns:
+                begin = START[q] - START[turns[0]]
+                packed[q, 0 : SIZE[q], cols] = block[begin : begin + SIZE[q]]
+                if ORDER[q] not in POOLED:
                     land = yin if ORDER[q] == 0 else mid
-                    land[q, 0:PAIR, cols] = block[begin[i] : begin[i] + PAIR]
-        if k == 0:
+                    land[q, 0:PAIR, cols] = block[begin : begin + PAIR]
+        if first:
             pl.semaphore_wait(barrier, len(peers))
-        for i in range(2):
-            q = 2 * k + i
-            if i in pooled:
-                peer = at_yz(0, ORDER[q])
-                send(m_copies, q, remote(meta_out.at[q], meta_in.at[q], m_ss.at[q], m_rs.at[q], peer))
+        for q in turns:
+            if ORDER[q] in POOLED:
                 send(z_copies, q, remote(
-                    packed.at[q, span], mid.at[q, span], z_ss.at[q], z_rs.at[q], peer
+                    packed.at[q, span], mid.at[q, span], z_ss.at[q], z_rs.at[q],
+                    at_yz(0, ORDER[q]),
                 ))
                 continue
             land = yin if ORDER[q] == 0 else mid
@@ -167,6 +163,18 @@
                     packed.at[q, half(d)], land.at[q, half(d)],
                     y_ss.at[q, d - 1], y_rs.at[q, d - 1], at_yz(d, 0),
                 ))
+        pooled = [q for q in turns if ORDER[q] in POOLED]
+        if pooled:
+            codes = lax.dot_general(
+                jnp.broadcast_to(code[...], (8, rows)).astype(BF16), pick,
+                (((1,), (1,)), ((), ())), preferred_element_type=F32,
+            )
+        for q in pooled:
+            begin = START[q] - START[turns[0]]
+            meta_out[q, :, 0:SLOTS] = codes[:, begin : begin + SLOTS]
+            send(m_copies, q, remote(
+                meta_out.at[q], meta_in.at[q], m_ss.at[q], m_rs.at[q], at_yz(0, ORDER[q])
+            ))
 
     def forward(k):
         for q in (2 * k, 2 * k + 1):
@@ -355,6 +363,7 @@
 
     assign()
     pack(0)
+    pack(2, 3)
     dropped = jnp.where(tgt_row[...] < 0, 1.0, 0.0)
     flags[0] = jnp.broadcast_to(jnp.max(dropped, axis=1, keepdims=True), flags.shape[1:])
     for d in range(1, NZ):
@@ -364,9 +373,9 @@
     a_copy.start()
     for copy in base_copies(0, 0):
         copy.start()
+    pack(4, 5)
+    pack(6, 7)
     pack(1)
-    pack(2)
-    pack(3)
     rank_row = lax.broadcasted_iota(jnp.int32, up.shape, 0) % 128
     umat[:, 0:128] = jnp.where(rank_row < 64, up[...].astype(F32), 0.0).astype(BF16)
     umat[:, 128:256] = jnp.where(rank_row < 64, 0.0, up[...].astype(F32)).astype(BF16)
@@ -405,9 +414,9 @@
     expand(2)
     collect(0, False)
     reduce(3)
-    collect(1, False)
     expand(3)
     back(2)
+    collect(1, False)
     back(3)
     collect(2, False)
     collect(3, True)

time: 103 us -> 122 us (1.18)
  Pallas kernels: 99.4 us -> 118 us
    pallas_call x1, Pallas kernels: 99.4 us -> 118 us  [local(): pl.pallas_call(kernel, out_shape=(jax.ShapeDtypeStruct((rows, 2 * kv), BF...]
where the time goes in v6:
time: 122 us; the launch traced here: 121 us
  Pallas kernels  118 us (97%)
  local copies, waits for them, and re-layouts  1.42 us (1%)
    pallas_call x1, Pallas kernels, local(): pl.pallas_call(kernel, out_shape=(jax.ShapeDtypeStruct((rows, 2 * kv), BF...  118 us

profile of v6, /device:TPU:32, one launch (start us, length us, event | category | flops | bytes accessed | tf_op | source)
XLA Modules:
  0.0 120.8 jit_solution(11427349231767669266)
XLA Ops:
  0.0 0.0 copy-start.2
  0.0 0.0 copy-start.3
  0.0 0.0 copy-start.4
  0.0 118.4 %shard_map.66 = (bf16[1024,256]{1,0:T(8,128)(2,1)S(1)}, f32[1,1]{1,0:T(1,128)}) custom-call(s32[1,1024]{1,0:T(1,128)} %bitcast.65, s32[1,256]{1,0:T(1,128)} %bitcast.67, bf16[1024,128]{1,0:T(8,128)(2,1)} %bitcast.60, bf16[1024,8192]{1,0:T(8,128)(2,1)} %tokens.1, bf16[16384,128]{1,0:T(8,128)(2,1)} %bitcast.56, bf16[8,1024,128]{2,1,0:T(8,128)(2,1)} %down.1), custom_call_target="tpu_custom_call" | custom-call | flops 12000000000 | bytes 24000000 | tf_op jit(solution)/shard_map/pallas_call | solution.py:478
  119.1 0.0 copy-done.2
  119.1 0.0 copy-done.3
  119.2 0.0 copy-done.4
  119.2 0.9 conditional.1
  119.2 0.2 copy.36
  119.4 0.4 copy.41
  120.0 0.0 copy-start.1
  120.1 0.8 copy-done.1
Async XLA Ops:
  0.0 119.1 %copy-start.2 = (bf16[8,2,64,128]{3,2,1,0:T(8,128)(2,1)S(1)}, bf16[8,2,64,128]{3,2,1,0:T(8,128)(2,1)}, u32[]{:S(2)}) copy-start(bf16[8,2,64,128]{3,2,1,0:T(8,128)(2,1)} %param.13) | copy-start | bytes 786436
  0.0 119.1 %copy-start.3 = (s32[1024,1]{0,1:T(1,128)S(1)}, s32[1024,1]{0,1:T(1,128)}, u32[]{:S(2)}) copy-start(s32[1024,1]{0,1:T(1,128)} %param.9) | copy-start | bytes 12292
  0.0 119.2 %copy-start.4 = (s32[256]{0:T(256)S(1)}, s32[256]{0:T(256)}, u32[]{:S(2)}) copy-start(s32[256]{0:T(256)} %param.10) | copy-start | bytes 3076
  120.0 0.8 copy-start.1
